TPU v7x, 128 devices: a whole 4x4x4 slice. The times are simulated.
128 devices in a mesh: retr: 8 (over y, core), store: 16 (over x, z).
Axes of the slice: x: 4, y: 4, z: 4, core: 2. Of those that a mesh axis runs over, the one named last changes fastest.
Arguments:
- tokens: bfloat16 [4096, 8192], P('retr', 'store'), may hold values from -6 to 6
- norm_gain: float32 [8192], replicated, may hold values from 0.1 to 1.9
- query_weight: bfloat16 [8192, 8192], P(None, 'store'), may hold values from -1 to 1
- kv_weight: bfloat16 [896, 2, 8192], P('store'), may hold values from -4 to 4
- out_weight: bfloat16 [8192, 8192], P('store'), may hold values from -0.0625 to 0.0625
- neighbour_pool: bfloat16 [128, 128, 896], P('retr'), may hold values from -6 to 6
- neighbour_shard: int32 [64, 2], P('retr'), may hold values from 0 to 7, all different within a row; in each aligned block of 8 rows (0 to 7, 8 to 15, ...) at most 2 rows name the same one
- neighbour_slot: int32 [64, 2], P('retr'), may hold values from 0 to 15
Outputs:
- mixed: bfloat16 [4096, 8192], P('retr', 'store')
Inputs may be any that keep to these rules, and one draw needn't show every extreme that they name: `neighbour_shard`: the 2 neighbours of a span lie on different shards. Among the 8 spans of one aligned block (the spans of one index of retr), no shard is named more than 2 times, and in some block one shard is named exactly 2 times.
All inputs are finite; a program needn't handle non-finite values.
Results may differ from a plain program's by a relative error of at most 0.0095.
Values may be sent and summed in bfloat16 or wider, within the bound.
A program may use at most 192 MiB of HBM per device.

v0:
```python
import jax
import jax.numpy as jnp
from jax import lax
from jax.sharding import PartitionSpec as P

DH = 128
ENC = 896
SPAN = 64
NL = 128
NEIGH = 2


def on_device(
    tokens,
    norm_gain,
    query_weight,
    kv_weight,
    out_weight,
    neighbour_pool,
    neighbour_shard,
    neighbour_slot,
):
    n_retr = lax.axis_size("retr")
    tok_rows = tokens.shape[0]
    spans_here = tok_rows // SPAN
    head_cols = query_weight.shape[1]
    heads_here = head_cols // DH
    capacity = max(2, (NEIGH * spans_here + n_retr - 1) // n_retr)
    whole = lax.all_gather(tokens, "store", axis=1, tiled=True)
    xf = whole.astype(jnp.float32)
    normed = (
        xf * lax.rsqrt(jnp.mean(xf * xf, axis=-1, keepdims=True) + 1e-05) * norm_gain[None, :]
    ).astype(jnp.bfloat16)
    query = (
        jnp.dot(normed, query_weight, preferred_element_type=jnp.float32) * DH ** (-0.5)
    ).astype(jnp.bfloat16)
    own_kv = lax.all_to_all(kv_weight, "store", split_axis=2, concat_axis=0, tiled=True)
    shard_flat = neighbour_shard.reshape(-1)
    slot_flat = neighbour_slot.reshape(-1)
    onehot = (shard_flat[:, None] == jnp.arange(n_retr, dtype=jnp.int32)[None, :]).astype(jnp.int32)
    before = jnp.cumsum(onehot, axis=0) - onehot
    position = jnp.sum(before * onehot, axis=1)
    request = jnp.zeros((n_retr, capacity), jnp.int32).at[shard_flat, position].set(slot_flat)
    asked = lax.all_to_all(request, "retr", split_axis=0, concat_axis=0, tiled=True)
    picked = neighbour_pool[asked.reshape(-1)].reshape(n_retr, capacity, NL, ENC)
    fetched = lax.all_to_all(picked, "retr", split_axis=0, concat_axis=0, tiled=True)
    context = fetched[shard_flat, position].reshape(spans_here, NEIGH * NL, ENC)
    kv = jnp.einsum("cke,esf->cksf", context, own_kv, preferred_element_type=jnp.float32).astype(
        jnp.bfloat16
    )
    kv = kv.reshape(spans_here, NEIGH * NL, 2, heads_here, DH)
    keys = kv[:, :, 0]
    values = kv[:, :, 1]
    query_heads = query.reshape(spans_here, SPAN, heads_here, DH)
    scores = jnp.einsum("cqhd,ckhd->chqk", query_heads, keys, preferred_element_type=jnp.float32)
    weights = jax.nn.softmax(scores, axis=-1).astype(jnp.bfloat16)
    attended = jnp.einsum("chqk,ckhd->cqhd", weights, values, preferred_element_type=jnp.float32)
    attended = attended.reshape(tok_rows, head_cols).astype(jnp.bfloat16)
    partial_value = jnp.dot(attended, out_weight, preferred_element_type=jnp.float32)
    summed = lax.psum_scatter(
        partial_value.astype(jnp.bfloat16), "store", scatter_dimension=1, tiled=True
    ).astype(jnp.float32)
    return (tokens.astype(jnp.float32) + summed).astype(jnp.bfloat16)


def solution(mesh):
    return jax.shard_map(
        on_device,
        mesh=mesh,
        in_specs=(
            P("retr", "store"),
            P(),
            P(None, "store"),
            P("store", None, None),
            P("store", None),
            P("retr", None, None),
            P("retr", None),
            P("retr", None),
        ),
        out_specs=P("retr", "store"),
        check_vma=False,
    )
```

profile of v0, /device:TPU:1, one launch (start us, length us, event | category | flops | bytes accessed | tf_op | source)
XLA Modules:
  0.0 287.5 jit_solution(6070398009698303379)
XLA Ops:
  6.5 0.7 all-gather.2.cloned.1.call-update
  7.3 0.8 copy.36
  8.2 0.8 copy.38
  9.1 0.2 select_reduce_fusion
  9.3 1.3 scatter_fusion
  10.6 0.7 copy.39
  11.3 6.0 %all-to-all-start = ((s32[8,1,2]{2,1,0:T(1,128)}), s32[8,1,2]{2,1,0:T(1,128)S(1)}, u32[]{:S(2)}, u32[]{:S(2)}) async-start(s32[8,1,2]{2,1,0:T(1,128)} %copy.39), calls=%async_computation | async-start | bytes 8192 | tf_op jit(solution)/shard_map/all_to_all | solution.py:44
  17.3 11.4 %copy.40 = bf16[56,2,8192]{0,1,2:T(2,128)(2,1)} copy(bf16[56,2,8192]{2,1,0:T(2,128)(2,1)} %param.11) | data formatting | bytes 3670016 | tf_op args[3]
  28.7 17.6 %reshape.145 = bf16[16,2,28672]{2,1,0:T(2,128)(2,1)} reshape(bf16[8192,2,56]{2,1,0:T(2,128)(2,1)} %bitcast.57) | data formatting | bytes 3670016
  46.3 7.6 %all-to-all-start.2 = ((bf16[16,2,28672]{2,1,0:T(2,128)(2,1)}), bf16[16,2,28672]{2,1,0:T(2,128)(2,1)S(1)}, u32[]{:S(2)}, u32[]{:S(2)}) async-start(bf16[16,2,28672]{2,1,0:T(2,128)(2,1)} %reshape.145), calls=%async_computation.2 | async-start | bytes 3670016 | tf_op jit(solution)/shard_map/all_to_all | solution.py:37
  53.9 0.5 broadcast.147
  54.4 0.7 reduce.3
  55.2 4.8 %gather_fusion = bf16[16,128,896]{2,1,0:T(8,128)(2,1)} fusion(bf16[16,128,896]{2,1,0:T(8,128)(2,1)} %param.13, s32[1024]{0:T(1024)S(1)} %pad_clamp_fusion), kind=kCustom, calls=%fused_computation | custom fusion | bytes 7340096 | tf_op jit(solution)/shard_map/gather | solution.py:45
  60.0 26.6 %all-to-all-done.2 = bf16[16,2,28672]{2,1,0:T(2,128)(2,1)S(1)} async-done(((bf16[16,2,28672]{2,1,0:T(2,128)(2,1)}), bf16[16,2,28672]{2,1,0:T(2,128)(2,1)S(1)}, u32[]{:S(2)}, u32[]{:S(2)}) %all-to-all-start.2) | async-done | bytes 1835040 | tf_op jit(solution)/shard_map/all_to_all | solution.py:37
  86.6 5.8 %all-to-all-start.1 = ((bf16[8,2,128,896]{3,2,1,0:T(8,128)(2,1)}), bf16[8,2,128,896]{3,2,1,0:T(8,128)(2,1)}, u32[]{:S(2)}, u32[]{:S(2)}) async-start(bf16[8,2,128,896]{3,2,1,0:T(8,128)(2,1)} %bitcast.58), calls=%async_computation.1 | async-start | bytes 7340032 | tf_op jit(solution)/shard_map/all_to_all | solution.py:46
  92.4 8.5 %reshape.146 = bf16[8192,2,56]{2,1,0:T(2,128)(2,1)} reshape(bf16[16,2,28672]{2,1,0:T(2,128)(2,1)S(1)} %all-to-all-done.2) | data formatting | bytes 3670016
  100.9 9.1 %copy.41 = bf16[56,2,16,512]{3,0,2,1:T(8,128)(2,1)S(1)} copy(bf16[56,2,16,512]{0,1,3,2:T(2,128)(2,1)} %bitcast.56) | data formatting | bytes 3670016 | tf_op jit(solution)/shard_map/all_to_all | solution.py:37
  110.0 25.7 %all-to-all-done.1 = bf16[8,2,128,896]{3,2,1,0:T(8,128)(2,1)} async-done(((bf16[8,2,128,896]{3,2,1,0:T(8,128)(2,1)}), bf16[8,2,128,896]{3,2,1,0:T(8,128)(2,1)}, u32[]{:S(2)}, u32[]{:S(2)}) %all-to-all-start.1) | async-done | bytes 3670048 | tf_op jit(solution)/shard_map/all_to_all | solution.py:46
  135.7 4.9 %gather_fusion.1 = bf16[16,128,896]{2,1,0:T(8,128)(2,1)} fusion(bf16[8,2,128,896]{3,2,1,0:T(8,128)(2,1)} %all-to-all-done.1, s32[16]{0:T(128)S(1)} %bitcast.62), kind=kCustom, calls=%fused_computation.1 | custom fusion | bytes 7340160 | tf_op jit(solution)/shard_map/gather | solution.py:47
  140.6 8.1 %convolution_convert_fusion.1 = bf16[8,256,2,512]{3,1,2,0:T(8,128)(2,1)} fusion(bf16[8,256,896,1]{2,1,3,0:T(8,128)(2,1)} %bitcast.59, bf16[896,2,512,1]{2,0,1,3:T(8,128)(2,1)S(1)} %bitcast.60), kind=kOutput, calls=%fused_computation.13 | convolution fusion | flops 3760193536 | bytes 9699328 | tf_op jit(solution)/shard_map/cke,esf->cksf/dot_general | solution.py:48
  148.7 6.9 %reshape.112 = bf16[8,256,2,4,128]{4,3,1,2,0:T(4,128)(2,1)} reshape(bf16[8,256,2,512]{3,1,2,0:T(8,128)(2,1)} %convolution_convert_fusion.1) | data formatting | bytes 8388608 | tf_op jit(solution)/shard_map/reshape | solution.py:51
  155.6 4.4 %fusion.28 = (bf16[8,256,1,4,128]{4,3,1,2,0:T(4,128)(2,1)}, bf16[8,256,1,4,128]{4,3,1,2,0:T(4,128)(2,1)}) fusion(bf16[8,256,2,4,128]{4,3,1,2,0:T(4,128)(2,1)} %reshape.112), kind=kLoop, calls=%fused_computation.44 | loop fusion | bytes 8388608 | tf_op jit(solution)/shard_map/slice | solution.py:52
  160.0 5.3 %fusion.1 = f32[512]{0:T(512)S(1)} fusion(bf16[512,8192]{1,0:T(8,128)(2,1)} %all-gather.2.cloned.1.call-done), kind=kLoop, calls=%fused_computation.6 | loop fusion | flops 12582400 | bytes 8390656 | tf_op jit(solution)/shard_map/reduce_sum | solution.py:32
  165.3 0.5 copy-done
  165.8 8.0 %fusion.14 = bf16[512,512]{1,0:T(8,128)(2,1)S(1)} fusion(bf16[8192,512]{1,0:T(8,128)(2,1)} %param.10, bf16[512,8192]{1,0:T(8,128)(2,1)S(1)} %copy-done, f32[8192]{0:T(1024)S(1)} %copy-done.2, f32[512]{0:T(512)S(1)} %add_rsqrt_fusion), kind=kOutput, calls=%fused_computation.22 | convolution fusion | flops 4312268800 | bytes 17336320 | tf_op jit(solution)/shard_map/dot_general | solution.py:35
  173.9 2.4 fusion.9
  176.3 0.6 fusion.29
  177.0 5.2 %fusion.17 = bf16[8,64,4,128]{3,1,2,0:T(8,128)(2,1)S(1)} fusion(bf16[8,256,1,4,128]{4,3,1,2,0:T(4,128)(2,1)} %get-tuple-element.8, f32[8,4,64]{2,1,0:T(4,128)S(1)} %fusion.29, f32[8,4,64,256]{3,2,1,0:T(8,128)S(1)} %fusion.9), kind=kOutput, calls=%fused_computation.23 | convolution fusion | flops 136055040 | bytes 4726784 | tf_op jit(solution)/shard_map/chqk,ckhd->cqhd/dot_general | solution.py:57
  182.2 0.4 copy.45
  182.6 10.1 %convolution_convert_fusion = bf16[512,8192]{1,0:T(8,128)(2,1)} fusion(bf16[512,8192]{1,0:T(8,128)(2,1)} %param.12, bf16[64,8,4,128]{3,2,1,0:T(4,128)(2,1)S(1)} %bitcast.61), kind=kOutput, calls=%fused_computation.9 | convolution fusion | flops 4299161600 | bytes 17301504 | tf_op jit(solution)/shard_map/dot_general | solution.py:59
  192.8 85.9 %reduce-scatter.2.cloned.1.call-done = bf16[512,512]{1,0:T(8,128)(2,1)} async-done(((bf16[512,8192]{1,0:T(8,128)(2,1)}), bf16[512,512]{1,0:T(8,128)(2,1)}) %reduce-scatter.2.cloned.1.call-update) | async-done | bytes 524304 | tf_op jit(solution)/shard_map/reduce_scatter | solution.py:60
  278.7 2.0 add_convert_fusion
  (22 shorter events, 0.6 us)
Async XLA Ops:
  6.5 153.5 %all-gather.2.cloned.1.call-start = ((), (), s32[]{:S(2)}) async-start(), calls=%async_computation.4 | async-start | bytes 8912896 | tf_op jit(solution)/shard_map/all_gather | solution.py:29
  11.3 35.0 %all-to-all-start = ((s32[8,1,2]{2,1,0:T(1,128)}), s32[8,1,2]{2,1,0:T(1,128)S(1)}, u32[]{:S(2)}, u32[]{:S(2)}) async-start(s32[8,1,2]{2,1,0:T(1,128)} %copy.39), calls=%async_computation | async-start | bytes 8192 | tf_op jit(solution)/shard_map/all_to_all | solution.py:44
  46.3 40.4 %all-to-all-start.2 = ((bf16[16,2,28672]{2,1,0:T(2,128)(2,1)}), bf16[16,2,28672]{2,1,0:T(2,128)(2,1)S(1)}, u32[]{:S(2)}, u32[]{:S(2)}) async-start(bf16[16,2,28672]{2,1,0:T(2,128)(2,1)} %reshape.145), calls=%async_computation.2 | async-start | bytes 3670016 | tf_op jit(solution)/shard_map/all_to_all | solution.py:37
  86.6 49.1 %all-to-all-start.1 = ((bf16[8,2,128,896]{3,2,1,0:T(8,128)(2,1)}), bf16[8,2,128,896]{3,2,1,0:T(8,128)(2,1)}, u32[]{:S(2)}, u32[]{:S(2)}) async-start(bf16[8,2,128,896]{3,2,1,0:T(8,128)(2,1)} %bitcast.58), calls=%async_computation.1 | async-start | bytes 7340032 | tf_op jit(solution)/shard_map/all_to_all | solution.py:46
  92.4 186.3 %reduce-scatter.2.cloned.1.call-start = ((), (), s32[]{:S(2)}) async-start(), calls=%async_computation.5 | async-start | bytes 8912896 | tf_op jit(solution)/shard_map/reduce_scatter | solution.py:60
  155.6 9.6 %copy-start.2 = (f32[8192]{0:T(1024)S(1)}, f32[8192]{0:T(1024)}, u32[]{:S(2)}) copy-start(f32[8192]{0:T(1024)} %param.9) | copy-start | bytes 98308
  160.0 5.8 %copy-start = (bf16[512,8192]{1,0:T(8,128)(2,1)S(1)}, bf16[512,8192]{1,0:T(8,128)(2,1)}, u32[]{:S(2)}) copy-start(bf16[512,8192]{1,0:T(8,128)(2,1)} %all-gather.2.cloned.1.call-done) | copy-start | bytes 25165828
  192.8 86.0 %copy-start.1 = (bf16[512,512]{1,0:T(8,128)(2,1)S(1)}, bf16[512,512]{1,0:T(8,128)(2,1)}, u32[]{:S(2)}) copy-start(bf16[512,512]{1,0:T(8,128)(2,1)} %param.8) | copy-start | bytes 1572868
Sparse Core Ops, SparseCore 0:
  9.5 100.4 all-gather.1
  192.9 85.7 reduce-scatter.1
where the time goes:
time: 289 us; the launch traced here: 288 us
  waiting for transfers between devices  139 us (48%)
  local copies, waits for them, and re-layouts  72.9 us (25%)
  matrix products  33.9 us (12%)
  starting transfers between devices  19.4 us (7%)
  between operations  13.5 us (5%)
  other arithmetic  8.84 us (3%)
    reduce_scatter x1, waiting for transfers between devices, on_device(): lax.psum_scatter(partial_value.astype(jnp.bfloat16), 'store', scatter_dim...  85.9 us
    unnamed x11, local copies, waits for them, and re-layouts  39.5 us
    all_to_all x1, waiting for transfers between devices, on_device(): lax.all_to_all(kv_weight, 'store', split_axis=2, concat_axis=0, tiled=True)  26.6 us
    all_to_all x1, waiting for transfers between devices, on_device(): lax.all_to_all(picked, 'retr', split_axis=0, concat_axis=0, tiled=True)  25.7 us
    dot_general x1, matrix products, on_device(): jnp.dot(attended, out_weight, preferred_element_type=jnp.float32)  10.1 us
    all_to_all x1, local copies, waits for them, and re-layouts, on_device(): lax.all_to_all(kv_weight, 'store', split_axis=2, concat_axis=0, tiled=True)  9.08 us
    dot_general x1, matrix products, on_device(): jnp.einsum('cke,esf->cksf', context, own_kv, preferred_element_type=jnp.f...  8.12 us
    dot_general x1, matrix products, on_device(): jnp.dot(normed, query_weight, preferred_element_type=jnp.float32)  7.98 us
  transfers between devices with their start and end apart: 5, of which 3 were waited for; matrix products, arithmetic and copies ran while one was open for 28% of the time, Pallas kernels for 0%

commit v1 on v0

v1 whole, which is shorter than its diff:
```python
import jax
import jax.numpy as jnp
from jax import lax
from jax.experimental import pallas as pl
from jax.experimental.pallas import tpu as pltpu
from jax.sharding import PartitionSpec as P

MESH = pl.DeviceIdType.MESH
BF16, F32, I32 = jnp.bfloat16, jnp.float32, jnp.int32

DH, ENC, SPAN, NL, NEIGH = 128, 896, 64, 128, 2
D, HC, ROWS, HALF, QUART = 8192, 512, 512, 256, 128
EROWS, EPAD = 56, 64
STEP = (0, 1, -1, 2)


def _dot(a, b):
    return jnp.dot(a, b, preferred_element_type=F32)


def kernel(
    tok_ref, gain_ref, shard_ref, slot_ref, wq_hbm, kvw_hbm, wo_hbm, pool_hbm, out_ref,
    slots, wq, acc, ssq, pool, picked, fetched, keys, values, kvraw, kvsend, kvrecv, w32, wkv,
    reqs, table, table_s, place_s, att, wo, send1, recv1h, recv1, send2, recv2h, recv2,
    load_sem, raw_sem, ag_send, ag_recv, req_send, req_recv, kv_send, kv_recv,
    wy_send, wy_recv, pool_send, pool_recv, rs1h_send, rs1h_recv, rs1_send, rs1_recv,
    rs2_send, rs2_recv,
):
    retr, store = lax.axis_index("retr"), lax.axis_index("store")
    x, z = store // 4, store % 4
    y, c = retr // 2, retr % 2

    def device(dx, dy, dz, dc):
        return ((y + dy + 4) % 4 * 2 + (c + dc) % 2, (x + dx + 4) % 4 * 4 + (z + dz + 4) % 4)

    def along(kind, axis, step):
        return device(step, 0, 0, 0) if (kind == 0) == (axis == 1) else device(0, 0, step, 0)

    def column(kind, a, b):
        dx = jnp.where(kind == 0, a, b)
        dz = jnp.where(kind == 0, b, a)
        return (x + dx + 4) % 4 * 4 + (z + dz + 4) % 4

    def offset(i):
        return jnp.where(i == 0, 0, jnp.where(i == 1, 1, jnp.where(i == 2, -1, 2)))

    loads = [
        pltpu.make_async_copy(tok_ref.at[pl.ds(0, HALF)], slots.at[0, 0, 0], load_sem.at[0]),
        pltpu.make_async_copy(tok_ref.at[pl.ds(HALF, HALF)], slots.at[1, 0, 0], load_sem.at[1]),
        pltpu.make_async_copy(pool_hbm, pool, load_sem.at[2]),
        pltpu.make_async_copy(wq_hbm, wq, load_sem.at[3]),
        pltpu.make_async_copy(wo_hbm, wo, load_sem.at[4]),
    ]
    loads[0].start()
    loads[1].start()
    raws = [
        pltpu.make_async_copy(
            kvw_hbm.at[:, :, pl.ds(s * HC + y * DH, DH)], kvraw.at[s], raw_sem.at[s]
        )
        for s in range(16)
    ]
    for copy in raws:
        copy.start()
    for copy in loads[2:]:
        copy.start()

    barrier = pltpu.get_barrier_semaphore()
    for o in range(1, 16):
        pl.semaphore_signal(
            barrier, inc=1, device_id=(retr, (store + o) % 16), device_id_type=MESH
        )
    for o in range(1, 8):
        pl.semaphore_signal(barrier, inc=1, device_id=((retr + o) % 8, store), device_id_type=MESH)
    reqs[...] = jnp.zeros((8, 128), I32)
    reqs[:, 0:2] = shard_ref[...]
    reqs[:, 2:4] = slot_ref[...]
    pl.semaphore_wait(barrier, 22)

    RET = [(o // 2, o % 2) for o in range(8)]
    ORDER = [2, 6, 3, 7, 4, 5, 1]

    def peer_from(o):
        dy, dc = RET[o]
        return (y - dy + 4) % 4 * 2 + (c + dc) % 2

    req_msg = {}
    for o in ORDER:
        req_msg[o] = pltpu.make_async_remote_copy(
            reqs, table.at[retr], req_send.at[o], req_recv.at[o],
            device_id=device(0, RET[o][0], 0, RET[o][1]), device_id_type=MESH,
        )
        req_msg[o].start()

    def gather_msg(k, i, j, h):
        axis = 2 if j else 1
        move = j if j else i
        if move == 3:
            src_move, step, half = (1, -1, 0) if h == 0 else (2, 1, 1)
            src = (i, src_move) if j else (src_move, 0)
            rows = pl.ds(half * QUART, QUART)
            return pltpu.make_async_remote_copy(
                slots.at[k, src[0], src[1], rows], slots.at[k, i, j, rows],
                ag_send.at[k, i, j, h], ag_recv.at[k, i, j, h],
                device_id=along(k, axis, step), device_id_type=MESH,
            )
        src = (i, 0) if j else (0, 0)
        step = -1 if move == 1 else 1
        return pltpu.make_async_remote_copy(
            slots.at[k, src[0], src[1]], slots.at[k, i, j],
            ag_send.at[k, i, j, 0], ag_recv.at[k, i, j, 0],
            device_id=along(k, axis, step), device_id_type=MESH,
        )

    started = []

    def go(k, i, j, h=0):
        msg = gather_msg(k, i, j, h)
        msg.start()
        started.append(msg)

    def came(k, i, j, h=0):
        gather_msg(k, i, j, h).wait_recv()

    loads[0].wait()
    loads[1].wait()
    for k in range(2):
        go(k, 1, 0)
        go(k, 2, 0)
    for k in range(2):
        go(k, 0, 1)
        go(k, 0, 2)

    acc[...] = jnp.zeros((ROWS, HC), F32)
    ssq[...] = jnp.zeros((ROWS, 128), F32)

    def query_block(k, i, j):
        s = column(k, offset(i), offset(j))
        rows = pl.ds(k * HALF, HALF)
        xf = slots[k, i, j].astype(F32)
        sq = xf * xf
        ssq[rows, :] += (sq[:, 0:128] + sq[:, 128:256]) + (sq[:, 256:384] + sq[:, 384:512])
        g4 = gain_ref[s]
        g = jnp.concatenate([g4[t : t + 1, :] for t in range(4)], axis=1)
        acc[rows, :] += _dot((xf * g).astype(BF16), wq[pl.ds(pl.multiple_of(s * HC, HC), HC), :])

    def query_blocks(n, place):
        def body(t, carry):
            i, j = place(t // 2)
            query_block(t % 2, i, j)
            return carry

        lax.fori_loop(0, 2 * n, body, 0)

    for copy in raws:
        copy.wait()

    def split(s, carry):
        raw = kvraw[s].astype(F32)
        one = jnp.where(c == 0, raw[:, 0, :], raw[:, 1, :])
        kvsend[s] = jnp.concatenate([one, jnp.zeros((EPAD - EROWS, DH), F32)], axis=0).astype(BF16)
        return carry

    lax.fori_loop(0, 16, split, 0)
    kv_msg = []
    for o in range(1, 16):
        to = (store + o) % 16
        msg = pltpu.make_async_remote_copy(
            kvsend.at[to], kvrecv.at[store], kv_send.at[o], kv_recv.at[o],
            device_id=(retr, to), device_id_type=MESH,
        )
        msg.start()
        kv_msg.append(msg)
    kvrecv[store] = kvsend[store]

    table[retr] = reqs[...]
    for o in ORDER:
        req_msg[o].wait_recv()
    to_smem = pltpu.make_async_copy(table, table_s, load_sem.at[5])
    to_smem.start()
    to_smem.wait()
    loads[2].wait()
    pool_msg = {}
    for o in [*ORDER, 0]:
        dy, dc = RET[o]
        to = (y + dy) % 4 * 2 + (c + dc) % 2
        first, second, seen = I32(0), I32(0), I32(0)
        for n in range(16):
            hit = table_s[to, n // 2, n % 2] == retr
            slot = table_s[to, n // 2, 2 + n % 2]
            first = jnp.where(hit & (seen == 0), slot, first)
            second = jnp.where(hit & (seen == 1), slot, second)
            seen = seen + jnp.where(hit, 1, 0)
        if o == 0:
            fetched[2 * retr] = pool[first]
            fetched[2 * retr + 1] = pool[second]
            continue
        picked[2 * o] = pool[first]
        picked[2 * o + 1] = pool[second]
        pool_msg[o] = pltpu.make_async_remote_copy(
            picked.at[pl.ds(2 * o, 2)], fetched.at[pl.ds(2 * retr, 2)],
            pool_send.at[o], pool_recv.at[o],
            device_id=device(0, dy, 0, dc), device_id_type=MESH,
        )
        pool_msg[o].start()
    mine = [table_s[retr, n // 2, n % 2] for n in range(16)]
    for n in range(16):
        before = I32(0)
        for m in range(n):
            before = before + jnp.where(mine[m] == mine[n], 1, 0)
        place_s[n] = 2 * mine[n] + before

    loads[3].wait()
    query_blocks(1, lambda t: (0, 0))

    for k in range(2):
        came(k, 1, 0)
        go(k, 3, 0, 0)
        go(k, 1, 1)
        go(k, 1, 2)
        came(k, 2, 0)
        go(k, 3, 0, 1)
        go(k, 2, 1)
        go(k, 2, 2)
    query_blocks(2, lambda t: (1 + t, 0))

    for msg in kv_msg:
        msg.wait_recv()

    def assemble(s, carry):
        part = kvrecv[s].astype(F32)
        w32[pl.ds(pl.multiple_of(s * EROWS, 8), EROWS), :] = part[:EROWS]
        return carry

    lax.fori_loop(0, 16, assemble, 0)
    wkv[c, :, pl.ds(pl.multiple_of(y * DH, DH), DH)] = w32[...].astype(BF16)

    def weight_part(dy, dc):
        return wkv.at[(c + dc) % 2, :, pl.ds(pl.multiple_of((y - dy + 4) % 4 * DH, DH), DH)]

    def weight_msg(o):
        dy, dc = RET[o]
        if dc:
            return pltpu.make_async_remote_copy(
                weight_part(dy, 0), weight_part(dy, 0), wy_send.at[o], wy_recv.at[o],
                device_id=device(0, 0, 0, 1), device_id_type=MESH,
            )
        return pltpu.make_async_remote_copy(
            weight_part(0, 0), weight_part(0, 0), wy_send.at[o], wy_recv.at[o],
            device_id=device(0, dy, 0, 0), device_id_type=MESH,
        )

    wy_msg = {}

    def weight_go(o):
        wy_msg[o] = weight_msg(o)
        wy_msg[o].start()

    for o in (2, 6, 4, 1):
        weight_go(o)

    for k in range(2):
        came(k, 0, 1)
        go(k, 0, 3, 0)
        came(k, 0, 2)
        go(k, 0, 3, 1)
    query_blocks(2, lambda t: (0, 1 + t))
    for k in range(2):
        came(k, 3, 0, 0)
        came(k, 3, 0, 1)
        go(k, 3, 1)
        go(k, 3, 2)
    query_blocks(1, lambda t: (3, 0))
    for i in (1, 2):
        for k in range(2):
            came(k, i, 1)
            go(k, i, 3, 0)
            came(k, i, 2)
            go(k, i, 3, 1)
    query_blocks(4, lambda t: (1 + t // 2, 1 + t % 2))

    for o in (2, 6, 4):
        wy_msg[o].wait_recv()
        weight_go(o + 1)

    def kv_block(r):
        ctx = fetched[pl.ds(2 * r, 2)].reshape(2 * NL, ENC)
        keys[pl.ds(2 * r, 2)] = _dot(ctx, wkv[0]).astype(BF16).reshape(2, NL, HC)
        values[pl.ds(2 * r, 2)] = _dot(ctx, wkv[1]).astype(BF16).reshape(2, NL, HC)

    for k in range(2):
        came(k, 3, 1)
        go(k, 3, 3, 0)
        came(k, 3, 2)
        go(k, 3, 3, 1)
    query_blocks(2, lambda t: (3, 1 + t))
    for o in (1, 3, 5, 7):
        wy_msg[o].wait_recv()
    pool_msg[1].wait_recv()
    first_two = (retr, peer_from(1))
    lax.fori_loop(
        0, 2, lambda t, v: (kv_block(jnp.where(t == 0, first_two[0], first_two[1])), v)[1], 0
    )
    for k in range(2):
        for i in range(4):
            came(k, i, 3, 0)
            came(k, i, 3, 1)
    query_blocks(4, lambda t: (t, 3))
    for group in ((2, 6), (3, 7), (4, 5)):
        for o in group:
            pool_msg[o].wait_recv()
        pair = tuple(peer_from(o) for o in group)
        lax.fori_loop(
            0, 2, lambda t, v: (kv_block(jnp.where(t == 0, pair[0], pair[1])), v)[1], 0
        )

    def span(n, carry):
        rows = pl.ds(pl.multiple_of(n * SPAN, SPAN), SPAN)
        mean = jnp.sum(ssq[rows, :], axis=1, keepdims=True) * (1.0 / D)
        q = (acc[rows, :] * (lax.rsqrt(mean + 1e-05) * DH**-0.5)).astype(BF16)
        j0, j1 = place_s[2 * n], place_s[2 * n + 1]
        ks = jnp.concatenate([keys[j0], keys[j1]], axis=0)
        vs = jnp.concatenate([values[j0], values[j1]], axis=0)
        outs = []
        for h in range(4):
            cols = slice(h * DH, (h + 1) * DH)
            sc = lax.dot_general(
                q[:, cols], ks[:, cols], (((1,), (1,)), ((), ())), preferred_element_type=F32
            )
            e = jnp.exp(sc - jnp.max(sc, axis=1, keepdims=True))
            w = (e / jnp.sum(e, axis=1, keepdims=True)).astype(BF16)
            outs.append(_dot(w, vs[:, cols]).astype(BF16))
        att[rows, :] = jnp.concatenate(outs, axis=1)
        return carry

    lax.fori_loop(0, 8, span, 0)

    loads[4].wait()

    def block(k, a, b):
        s = column(k, a, b)
        return _dot(
            att[pl.ds(pl.multiple_of(k * HALF, HALF), HALF), :],
            wo[:, pl.ds(pl.multiple_of(s * HC, HC), HC)],
        )

    def one_h(k, i, h):
        return pltpu.make_async_remote_copy(
            send1.at[k, i, 0, pl.ds(h * QUART, QUART)], recv1h.at[k, i, h],
            rs1h_send.at[k, i, h], rs1h_recv.at[k, i, h],
            device_id=along(k, 2, 1 if h == 0 else -1), device_id_type=MESH,
        )

    def one(k, i, d):
        return pltpu.make_async_remote_copy(
            send1.at[k, i, 1 + d], recv1.at[k, i, d], rs1_send.at[k, i, d], rs1_recv.at[k, i, d],
            device_id=along(k, 2, 1 if d == 0 else -1), device_id_type=MESH,
        )

    def two_h(k, h):
        return pltpu.make_async_remote_copy(
            send2.at[k, 0, pl.ds(h * QUART, QUART)], recv2h.at[k, h],
            rs2_send.at[k, h], rs2_recv.at[k, h],
            device_id=along(k, 1, 1 if h == 0 else -1), device_id_type=MESH,
        )

    def two(k, d):
        return pltpu.make_async_remote_copy(
            send2.at[k, 1 + d], recv2.at[k, d], rs2_send.at[k, 2 + d], rs2_recv.at[k, 2 + d],
            device_id=along(k, 1, 1 if d == 0 else -1), device_id_type=MESH,
        )

    FAR = (3, 1, 2, 0)
    for i in FAR:
        for k in range(2):
            send1[k, i, 0] = block(k, STEP[i], 2).astype(BF16)
            for h in range(2):
                one_h(k, i, h).start()
    for i in FAR:
        for k in range(2):
            for d in range(2):
                one_h(k, i, d).wait_recv()
                part = block(k, STEP[i], 1 if d == 0 else -1)
                at = pl.ds(d * QUART, QUART)
                rest = pl.ds((1 - d) * QUART, QUART)
                got = recv1h[k, i, d].astype(F32)
                send1[k, i, 1 + d, at] = (part[d * QUART : (d + 1) * QUART] + got).astype(BF16)
                send1[k, i, 1 + d, rest] = part[(1 - d) * QUART : (2 - d) * QUART].astype(BF16)
                one(k, i, d).start()
    for i in FAR:
        for k in range(2):
            for d in range(2):
                one(k, i, d).wait_recv()
            total = block(k, STEP[i], 0) + recv1[k, i, 0].astype(F32) + recv1[k, i, 1].astype(F32)
            if i == 3:
                send2[k, 0] = total.astype(BF16)
                for h in range(2):
                    two_h(k, h).start()
            elif i:
                d = i - 1
                two_h(k, d).wait_recv()
                at = pl.ds(d * QUART, QUART)
                rest = pl.ds((1 - d) * QUART, QUART)
                got = recv2h[k, d].astype(F32)
                send2[k, 1 + d, at] = (total[d * QUART : (d + 1) * QUART] + got).astype(BF16)
                send2[k, 1 + d, rest] = total[(1 - d) * QUART : (2 - d) * QUART].astype(BF16)
                two(k, d).start()
            else:
                for d in range(2):
                    two(k, d).wait_recv()
                total = total + recv2[k, 0].astype(F32) + recv2[k, 1].astype(F32)
                own = slots[k, 0, 0].astype(F32)
                out_ref[pl.ds(k * HALF, HALF), :] = (own + total).astype(BF16)

    for msg in started:
        msg.wait_send()
    for msg in kv_msg:
        msg.wait_send()
    for o in ORDER:
        req_msg[o].wait_send()
        pool_msg[o].wait_send()
        wy_msg[o].wait_send()
    for k in range(2):
        for i in range(4):
            for d in range(2):
                one_h(k, i, d).wait_send()
                one(k, i, d).wait_send()
        for d in range(2):
            two_h(k, d).wait_send()
            two(k, d).wait_send()


def on_device(
    tokens, norm_gain, query_weight, kv_weight, out_weight, neighbour_pool, neighbour_shard, neighbour_slot
):
    gain = norm_gain.reshape(16, 4, 128)
    vmem, hbm = pl.BlockSpec(memory_space=pltpu.VMEM), pl.BlockSpec(memory_space=pl.ANY)
    dma = pltpu.SemaphoreType.DMA
    return pl.pallas_call(
        kernel,
        out_shape=jax.ShapeDtypeStruct((ROWS, HC), BF16),
        in_specs=[hbm, vmem, vmem, vmem, hbm, hbm, hbm, hbm],
        out_specs=vmem,
        scratch_shapes=[
            pltpu.VMEM((2, 4, 4, HALF, HC), BF16),
            pltpu.VMEM((D, HC), BF16),
            pltpu.VMEM((ROWS, HC), F32),
            pltpu.VMEM((ROWS, 128), F32),
            pltpu.VMEM((16, NL, ENC), BF16),
            pltpu.VMEM((16, NL, ENC), BF16),
            pltpu.VMEM((16, NL, ENC), BF16),
            pltpu.VMEM((16, NL, HC), BF16),
            pltpu.VMEM((16, NL, HC), BF16),
            pltpu.VMEM((16, EROWS, 2, DH), BF16),
            pltpu.VMEM((16, EPAD, DH), BF16),
            pltpu.VMEM((16, EPAD, DH), BF16),
            pltpu.VMEM((ENC, DH), F32),
            pltpu.VMEM((2, ENC, HC), BF16),
            pltpu.VMEM((8, 128), I32),
            pltpu.VMEM((8, 8, 128), I32),
            pltpu.SMEM((8, 8, 128), I32),
            pltpu.SMEM((16,), I32),
            pltpu.VMEM((ROWS, HC), BF16),
            pltpu.VMEM((HC, D), BF16),
            pltpu.VMEM((2, 4, 3, HALF, HC), BF16),
            pltpu.VMEM((2, 4, 2, QUART, HC), BF16),
            pltpu.VMEM((2, 4, 2, HALF, HC), BF16),
            pltpu.VMEM((2, 3, HALF, HC), BF16),
            pltpu.VMEM((2, 2, QUART, HC), BF16),
            pltpu.VMEM((2, 2, HALF, HC), BF16),
            dma((6,)), dma((16,)), dma((2, 4, 4, 2)), dma((2, 4, 4, 2)), dma((8,)), dma((8,)),
            dma((16,)), dma((16,)), dma((8,)), dma((8,)), dma((8,)), dma((8,)),
            dma((2, 4, 2)), dma((2, 4, 2)), dma((2, 4, 2)), dma((2, 4, 2)), dma((2, 4)), dma((2, 4)),
        ],
        compiler_params=pltpu.CompilerParams(
            collective_id=0, has_side_effects=True, vmem_limit_bytes=62 << 20
        ),
        cost_estimate=pl.CostEstimate(
            flops=13_000_000_000, bytes_accessed=24_000_000, transcendentals=600_000
        ),
        name="retro_block",
    )(tokens, gain, neighbour_shard, neighbour_slot, query_weight, kv_weight, out_weight, neighbour_pool)


def solution(mesh):
    return jax.shard_map(
        on_device,
        mesh=mesh,
        in_specs=(
            P("retr", "store"),
            P(),
            P(None, "store"),
            P("store", None, None),
            P("store", None),
            P("retr", None, None),
            P("retr", None),
            P("retr", None),
        ),
        out_specs=P("retr", "store"),
        check_vma=False,
    )
```

time: 289 us -> 143 us (0.49)
  waiting for transfers between devices: 139 us -> 0 us
  Pallas kernels: 0 us -> 136 us
  local copies, waits for them, and re-layouts: 72.9 us -> 4.56 us
  matrix products: 33.9 us -> 0 us
  starting transfers between devices: 19.4 us -> 0 us
  between operations: 13.5 us -> 0.01 us
  other arithmetic: 8.84 us -> 0 us
    pallas_call x0 -> x1, Pallas kernels: none -> 136 us  [on_device(): pl.pallas_call(kernel, out_shape=jax.ShapeDtypeStruct((ROWS, HC), BF16),...]
    reduce_scatter x1 -> x0, waiting for transfers between devices: 85.9 us -> none  [on_device(): lax.psum_scatter(partial_value.astype(jnp.bfloat16), 'store', scatter_dim...]
    all_to_all x3 -> x0, waiting for transfers between devices: 52.3 us -> none  [the longest x1 26.6 us: on_device(): lax.all_to_all(kv_weight, 'store', split_axis=2, concat_axis=0, tiled=True)]
    unnamed x11 -> x3, local copies, waits for them, and re-layouts: 39.5 us -> 4.56 us
    dot_general x5 -> x0, matrix products: 33.9 us -> none  [the longest x1 10.1 us: on_device(): jnp.dot(attended, out_weight, preferred_element_type=jnp.float32)]
    all_to_all x3 -> x0, starting transfers between devices: 19.4 us -> none  [the longest x1 7.63 us: on_device(): lax.all_to_all(kv_weight, 'store', split_axis=2, concat_axis=0, tiled=True)]
    all_to_all x3 -> x0, local copies, waits for them, and re-layouts: 10.3 us -> none  [the longest x1 9.08 us: on_device(): lax.all_to_all(kv_weight, 'store', split_axis=2, concat_axis=0, tiled=True)]
    gather x2 -> x0, local copies, waits for them, and re-layouts: 9.7 us -> none  [the longest x1 4.87 us: on_device(): context = fetched[shard_flat, position].reshape(spans_here, NEIGH * NL, ENC)]
  transfers between devices with their start and end apart: 5 -> 0, of which waited for: 3 -> 0; matrix products, arithmetic and copies ran while one was open for 28% -> 0% of each run, Pallas kernels for 0% -> 0%
where the time goes in v1:
time: 143 us; the launch traced here: 141 us
  Pallas kernels  136 us (95%)
  local copies, waits for them, and re-layouts  4.56 us (3%)
    pallas_call x1, Pallas kernels, on_device(): pl.pallas_call(kernel, out_shape=jax.ShapeDtypeStruct((ROWS, HC), BF16),...  136 us
    unnamed x3, local copies, waits for them, and re-layouts  4.56 us

profile of v1, /device:TPU:1, one launch (start us, length us, event | category | flops | bytes accessed | tf_op | source)
XLA Modules:
  0.0 140.8 jit_solution(14120447873286136586)
XLA Ops:
  0.0 1.3 copy.9.shard_ref
  1.3 1.3 copy.10.slot_ref
  2.7 136.3 %retro_block.1 = bf16[512,512]{1,0:T(8,128)(2,1)} custom-call(bf16[512,512]{1,0:T(8,128)(2,1)} %tok_ref.1, f32[16,4,128]{2,1,0:T(4,128)} %bitcast.1, s32[8,2]{1,0:T(8,128)} %copy.9.shard_ref, s32[8,2]{1,0:T(8,128)} %copy.10.slot_ref, bf16[8192,512]{1,0:T(8,128)(2,1)} %wq_hbm.1, bf16[56,2,8192]{2,1,0:T(2,128)(2,1)} %kvw_hbm.1, bf16[512,8192]{1,0:T(8,128)(2,1)} %wo_hbm.1, ...), custom_call_target="tpu_custom_call" | custom-call | flops 12999999488 | bytes 24000000 | tf_op jit(solution)/shard_map/retro_block/pallas_call | solution.py:438
  139.0 1.9 %copy.12 = bf16[512,512]{1,0:T(8,128)(2,1)} copy(bf16[512,512]{1,0:T(8,128)(2,1)} %retro_block.1) | data formatting | bytes 1048576

commit v2 on v1

--- a/solution.py
+++ b/solution.py
@@ -23,7 +23,7 @@
     slots, wq, acc, ssq, pool, picked, fetched, keys, values, kvraw, kvsend, kvrecv, w32, wkv,
     reqs, table, table_s, place_s, att, wo, send1, recv1h, recv1, send2, recv2h, recv2,
     load_sem, raw_sem, ag_send, ag_recv, req_send, req_recv, kv_send, kv_recv,
-    wy_send, wy_recv, pool_send, pool_recv, rs1h_send, rs1h_recv, rs1_send, rs1_recv,
+    wy_send, wy_recv, pool_send, pool_recv, share_send, share_recv, rs1h_send, rs1h_recv, rs1_send, rs1_recv,
     rs2_send, rs2_recv,
 ):
     retr, store = lax.axis_index("retr"), lax.axis_index("store")
@@ -72,12 +72,24 @@
     for o in range(1, 8):
         pl.semaphore_signal(barrier, inc=1, device_id=((retr + o) % 8, store), device_id_type=MESH)
     reqs[...] = jnp.zeros((8, 128), I32)
-    reqs[:, 0:2] = shard_ref[...]
-    reqs[:, 2:4] = slot_ref[...]
+    reqs[0:2, 0:8] = shard_ref[...]
+    reqs[2:4, 0:8] = slot_ref[...]
+
+    for copy in raws:
+        copy.wait()
+
+    def split(s, carry):
+        raw = kvraw[s].astype(F32)
+        one = jnp.where(c == 0, raw[:, 0, :], raw[:, 1, :])
+        kvsend[s] = jnp.concatenate([one, jnp.zeros((EPAD - EROWS, DH), F32)], axis=0).astype(BF16)
+        return carry
+
+    lax.fori_loop(0, 16, split, 0)
     pl.semaphore_wait(barrier, 22)
 
     RET = [(o // 2, o % 2) for o in range(8)]
-    ORDER = [2, 6, 3, 7, 4, 5, 1]
+    EARLY, LATE = [4, 5, 2, 6], [3, 7, 1]
+    ORDER = EARLY + LATE
 
     def peer_from(o):
         dy, dc = RET[o]
@@ -130,6 +142,17 @@
         go(k, 0, 1)
         go(k, 0, 2)
 
+    kv_msg = []
+    for o in range(1, 16):
+        to = (store + o) % 16
+        msg = pltpu.make_async_remote_copy(
+            kvsend.at[to], kvrecv.at[store], kv_send.at[o], kv_recv.at[o],
+            device_id=(retr, to), device_id_type=MESH,
+        )
+        msg.start()
+        kv_msg.append(msg)
+    kvrecv[store] = kvsend[store]
+
     acc[...] = jnp.zeros((ROWS, HC), F32)
     ssq[...] = jnp.zeros((ROWS, 128), F32)
 
@@ -151,27 +174,6 @@
 
         lax.fori_loop(0, 2 * n, body, 0)
 
-    for copy in raws:
-        copy.wait()
-
-    def split(s, carry):
-        raw = kvraw[s].astype(F32)
-        one = jnp.where(c == 0, raw[:, 0, :], raw[:, 1, :])
-        kvsend[s] = jnp.concatenate([one, jnp.zeros((EPAD - EROWS, DH), F32)], axis=0).astype(BF16)
-        return carry
-
-    lax.fori_loop(0, 16, split, 0)
-    kv_msg = []
-    for o in range(1, 16):
-        to = (store + o) % 16
-        msg = pltpu.make_async_remote_copy(
-            kvsend.at[to], kvrecv.at[store], kv_send.at[o], kv_recv.at[o],
-            device_id=(retr, to), device_id_type=MESH,
-        )
-        msg.start()
-        kv_msg.append(msg)
-    kvrecv[store] = kvsend[store]
-
     table[retr] = reqs[...]
     for o in ORDER:
         req_msg[o].wait_recv()
@@ -179,14 +181,26 @@
     to_smem.start()
     to_smem.wait()
     loads[2].wait()
+    def parity(o):
+        return (x if o == 4 else z) % 2
+
+    def share_msg(o):
+        at = pl.ds(2 * peer_from(o) + parity(o), 1)
+        step = 1 - 2 * ((parity(o) + c) % 2)
+        return pltpu.make_async_remote_copy(
+            fetched.at[at], fetched.at[at], share_send.at[o - 4], share_recv.at[o - 4],
+            device_id=device(step, 0, 0, 0) if o == 4 else device(0, 0, step, 0),
+            device_id_type=MESH,
+        )
+
     pool_msg = {}
     for o in [*ORDER, 0]:
         dy, dc = RET[o]
         to = (y + dy) % 4 * 2 + (c + dc) % 2
         first, second, seen = I32(0), I32(0), I32(0)
         for n in range(16):
-            hit = table_s[to, n // 2, n % 2] == retr
-            slot = table_s[to, n // 2, 2 + n % 2]
+            hit = table_s[to, n % 2, n // 2] == retr
+            slot = table_s[to, 2 + n % 2, n // 2]
             first = jnp.where(hit & (seen == 0), slot, first)
             second = jnp.where(hit & (seen == 1), slot, second)
             seen = seen + jnp.where(hit, 1, 0)
@@ -196,13 +210,15 @@
             continue
         picked[2 * o] = pool[first]
         picked[2 * o + 1] = pool[second]
+        n, skip = (1, parity(o)) if dy == 2 else (2, 0)
         pool_msg[o] = pltpu.make_async_remote_copy(
-            picked.at[pl.ds(2 * o, 2)], fetched.at[pl.ds(2 * retr, 2)],
+            picked.at[pl.ds(2 * o + skip, n)], fetched.at[pl.ds(2 * retr + skip, n)],
             pool_send.at[o], pool_recv.at[o],
             device_id=device(0, dy, 0, dc), device_id_type=MESH,
         )
-        pool_msg[o].start()
-    mine = [table_s[retr, n // 2, n % 2] for n in range(16)]
+        if o in EARLY:
+            pool_msg[o].start()
+    mine = [table_s[retr, n % 2, n // 2] for n in range(16)]
     for n in range(16):
         before = I32(0)
         for m in range(n):
@@ -257,6 +273,8 @@
 
     for o in (2, 6, 4, 1):
         weight_go(o)
+    for o in LATE:
+        pool_msg[o].start()
 
     for k in range(2):
         came(k, 0, 1)
@@ -278,61 +296,74 @@
             go(k, i, 3, 1)
     query_blocks(4, lambda t: (1 + t // 2, 1 + t % 2))
 
-    for o in (2, 6, 4):
-        wy_msg[o].wait_recv()
-        weight_go(o + 1)
-
-    def kv_block(r):
-        ctx = fetched[pl.ds(2 * r, 2)].reshape(2 * NL, ENC)
-        keys[pl.ds(2 * r, 2)] = _dot(ctx, wkv[0]).astype(BF16).reshape(2, NL, HC)
-        values[pl.ds(2 * r, 2)] = _dot(ctx, wkv[1]).astype(BF16).reshape(2, NL, HC)
-
+    for o in (4, 5):
+        pool_msg[o].wait_recv()
+        share_msg(o).start()
     for k in range(2):
         came(k, 3, 1)
         go(k, 3, 3, 0)
         came(k, 3, 2)
         go(k, 3, 3, 1)
     query_blocks(2, lambda t: (3, 1 + t))
+    for o in (2, 6, 4):
+        wy_msg[o].wait_recv()
+        weight_go(o + 1)
+
+    def kv_block(r):
+        ctx = fetched[pl.ds(2 * r, 2)].reshape(2 * NL, ENC)
+        turned = _dot(ctx, wkv[0]).astype(BF16).T
+        keys[2 * r] = turned[:, :NL]
+        keys[2 * r + 1] = turned[:, NL:]
+        values[pl.ds(2 * r, 2)] = _dot(ctx, wkv[1]).astype(BF16).reshape(2, NL, HC)
+
+
+    def kv_blocks(sources):
+        def body(t, carry):
+            r = sources[0]
+            for n in range(1, len(sources)):
+                r = jnp.where(t == n, sources[n], r)
+            kv_block(r)
+            return carry
+
+        lax.fori_loop(0, len(sources), body, 0)
+
     for o in (1, 3, 5, 7):
         wy_msg[o].wait_recv()
-    pool_msg[1].wait_recv()
-    first_two = (retr, peer_from(1))
-    lax.fori_loop(
-        0, 2, lambda t, v: (kv_block(jnp.where(t == 0, first_two[0], first_two[1])), v)[1], 0
-    )
-    for k in range(2):
-        for i in range(4):
+    for o in (2, 6):
+        pool_msg[o].wait_recv()
+    kv_blocks((retr, peer_from(2), peer_from(6)))
+    for k in range(2):
+        for i in range(3):
             came(k, i, 3, 0)
             came(k, i, 3, 1)
-    query_blocks(4, lambda t: (t, 3))
-    for group in ((2, 6), (3, 7), (4, 5)):
+    query_blocks(3, lambda t: (t, 3))
+    for k in range(2):
+        came(k, 3, 3, 0)
+        came(k, 3, 3, 1)
+    query_blocks(1, lambda t: (3, 3))
+    for group in ((4, 5), (1, 3, 7)):
         for o in group:
-            pool_msg[o].wait_recv()
-        pair = tuple(peer_from(o) for o in group)
-        lax.fori_loop(
-            0, 2, lambda t, v: (kv_block(jnp.where(t == 0, pair[0], pair[1])), v)[1], 0
-        )
+            if o in (4, 5):
+                share_msg(o).wait_recv()
+            else:
+                pool_msg[o].wait_recv()
+        kv_blocks(tuple(peer_from(o) for o in group))
 
     def span(n, carry):
         rows = pl.ds(pl.multiple_of(n * SPAN, SPAN), SPAN)
         mean = jnp.sum(ssq[rows, :], axis=1, keepdims=True) * (1.0 / D)
-        q = (acc[rows, :] * (lax.rsqrt(mean + 1e-05) * DH**-0.5)).astype(BF16)
+        scale = lax.rsqrt(mean + 1e-05) * DH**-0.5
         j0, j1 = place_s[2 * n], place_s[2 * n + 1]
-        ks = jnp.concatenate([keys[j0], keys[j1]], axis=0)
-        vs = jnp.concatenate([values[j0], values[j1]], axis=0)
-        outs = []
         for h in range(4):
             cols = slice(h * DH, (h + 1) * DH)
-            sc = lax.dot_general(
-                q[:, cols], ks[:, cols], (((1,), (1,)), ((), ())), preferred_element_type=F32
-            )
-            e = jnp.exp(sc - jnp.max(sc, axis=1, keepdims=True))
-            w = (e / jnp.sum(e, axis=1, keepdims=True)).astype(BF16)
-            outs.append(_dot(w, vs[:, cols]).astype(BF16))
-        att[rows, :] = jnp.concatenate(outs, axis=1)
+            q = (acc[rows, cols] * scale).astype(BF16)
+            s0, s1 = _dot(q, keys[j0, cols, :]), _dot(q, keys[j1, cols, :])
+            top = jnp.max(jnp.maximum(s0, s1), axis=1, keepdims=True)
+            e0, e1 = jnp.exp(s0 - top), jnp.exp(s1 - top)
+            weigh = 1.0 / jnp.sum(e0 + e1, axis=1, keepdims=True)
+            o = _dot(e0.astype(BF16), values[j0, :, cols]) + _dot(e1.astype(BF16), values[j1, :, cols])
+            att[rows, cols] = (o * weigh).astype(BF16)
         return carry
-
-    lax.fori_loop(0, 8, span, 0)
 
     loads[4].wait()
 
@@ -370,8 +401,9 @@
         )
 
     FAR = (3, 1, 2, 0)
-    for i in FAR:
-        for k in range(2):
+    for k in range(2):
+        lax.fori_loop(4 * k, 4 * k + 4, span, 0, unroll=4)
+        for i in FAR:
             send1[k, i, 0] = block(k, STEP[i], 2).astype(BF16)
             for h in range(2):
                 one_h(k, i, h).start()
@@ -419,6 +451,8 @@
         req_msg[o].wait_send()
         pool_msg[o].wait_send()
         wy_msg[o].wait_send()
+    for o in (4, 5):
+        share_msg(o).wait_send()
     for k in range(2):
         for i in range(4):
             for d in range(2):
@@ -448,7 +482,7 @@
             pltpu.VMEM((16, NL, ENC), BF16),
             pltpu.VMEM((16, NL, ENC), BF16),
             pltpu.VMEM((16, NL, ENC), BF16),
-            pltpu.VMEM((16, NL, HC), BF16),
+            pltpu.VMEM((16, HC, NL), BF16),
             pltpu.VMEM((16, NL, HC), BF16),
             pltpu.VMEM((16, EROWS, 2, DH), BF16),
             pltpu.VMEM((16, EPAD, DH), BF16),
@@ -468,7 +502,7 @@
             pltpu.VMEM((2, 2, QUART, HC), BF16),
             pltpu.VMEM((2, 2, HALF, HC), BF16),
             dma((6,)), dma((16,)), dma((2, 4, 4, 2)), dma((2, 4, 4, 2)), dma((8,)), dma((8,)),
-            dma((16,)), dma((16,)), dma((8,)), dma((8,)), dma((8,)), dma((8,)),
+            dma((16,)), dma((16,)), dma((8,)), dma((8,)), dma((8,)), dma((8,)), dma((2,)), dma((2,)),
             dma((2, 4, 2)), dma((2, 4, 2)), dma((2, 4, 2)), dma((2, 4, 2)), dma((2, 4)), dma((2, 4)),
         ],
         compiler_params=pltpu.CompilerParams(
@@ -478,7 +512,7 @@
             flops=13_000_000_000, bytes_accessed=24_000_000, transcendentals=600_000
         ),
         name="retro_block",
-    )(tokens, gain, neighbour_shard, neighbour_slot, query_weight, kv_weight, out_weight, neighbour_pool)
+    )(tokens, gain, neighbour_shard.T, neighbour_slot.T, query_weight, kv_weight, out_weight, neighbour_pool)
 
 
 def solution(mesh):

time: 143 us -> 120 us (0.84); the launches traced: 141 us -> 120 us
  Pallas kernels: 136 us -> 118 us
  local copies, waits for them, and re-layouts: 4.56 us -> 1.87 us
    pallas_call x1, Pallas kernels: 136 us -> 118 us  [on_device(): pl.pallas_call(kernel, out_shape=jax.ShapeDtypeStruct((ROWS, HC), BF16),...]
    unnamed x3 -> x1, local copies, waits for them, and re-layouts: 4.56 us -> 1.87 us
where the time goes in v2:
time: 120 us
  Pallas kernels  118 us (98%)
  local copies, waits for them, and re-layouts  1.87 us (2%)
    pallas_call x1, Pallas kernels, on_device(): pl.pallas_call(kernel, out_shape=jax.ShapeDtypeStruct((ROWS, HC), BF16),...  118 us

profile of v2, /device:TPU:1, one launch (start us, length us, event | category | flops | bytes accessed | tf_op | source)
XLA Modules:
  0.0 120.2 jit_solution(6408298139359373851)
XLA Ops:
  0.0 118.3 %retro_block.1 = bf16[512,512]{1,0:T(8,128)(2,1)} custom-call(bf16[512,512]{1,0:T(8,128)(2,1)} %tok_ref.1, f32[16,4,128]{2,1,0:T(4,128)} %bitcast.3, s32[2,8]{1,0:T(2,128)} %bitcast.4, s32[2,8]{1,0:T(2,128)} %bitcast.5, bf16[8192,512]{1,0:T(8,128)(2,1)} %wq_hbm.1, bf16[56,2,8192]{2,1,0:T(2,128)(2,1)} %kvw_hbm.1, bf16[512,8192]{1,0:T(8,128)(2,1)} %wo_hbm.1, ...), custom_call_target="tpu_custom_call" | custom-call | flops 12999999488 | bytes 24000000 | tf_op jit(solution)/shard_map/retro_block/pallas_call | solution.py:472
  118.4 1.9 %copy.10 = bf16[512,512]{1,0:T(8,128)(2,1)} copy(bf16[512,512]{1,0:T(8,128)(2,1)} %retro_block.1) | data formatting | bytes 1048576

commit v3 on v2

--- a/solution.py
+++ b/solution.py
@@ -19,10 +19,10 @@
 
 
 def kernel(
-    tok_ref, gain_ref, shard_ref, slot_ref, wq_hbm, kvw_hbm, wo_hbm, pool_hbm, out_ref,
+    tok_ref, gain_hbm, shard_hbm, slot_hbm, wq_hbm, kvw_hbm, wo_hbm, pool_hbm, out_ref,
     slots, wq, acc, ssq, pool, picked, fetched, keys, values, kvraw, kvsend, kvrecv, w32, wkv,
     reqs, table, table_s, place_s, att, wo, send1, recv1h, recv1, send2, recv2h, recv2,
-    load_sem, raw_sem, ag_send, ag_recv, req_send, req_recv, kv_send, kv_recv,
+    gain_ref, shard_ref, slot_ref, load_sem, raw_sem, ag_send, ag_recv, req_send, req_recv, kv_send, kv_recv,
     wy_send, wy_recv, pool_send, pool_recv, share_send, share_recv, rs1h_send, rs1h_recv, rs1_send, rs1_recv,
     rs2_send, rs2_recv,
 ):
@@ -51,8 +51,13 @@
         pltpu.make_async_copy(wq_hbm, wq, load_sem.at[3]),
         pltpu.make_async_copy(wo_hbm, wo, load_sem.at[4]),
     ]
-    loads[0].start()
-    loads[1].start()
+    small = [
+        pltpu.make_async_copy(shard_hbm, shard_ref, load_sem.at[6]),
+        pltpu.make_async_copy(slot_hbm, slot_ref, load_sem.at[7]),
+        pltpu.make_async_copy(gain_hbm, gain_ref, load_sem.at[8]),
+    ]
+    for copy in [*small, loads[0], loads[1]]:
+        copy.start()
     raws = [
         pltpu.make_async_copy(
             kvw_hbm.at[:, :, pl.ds(s * HC + y * DH, DH)], kvraw.at[s], raw_sem.at[s]
@@ -65,26 +70,16 @@
         copy.start()
 
     barrier = pltpu.get_barrier_semaphore()
-    for o in range(1, 16):
-        pl.semaphore_signal(
-            barrier, inc=1, device_id=(retr, (store + o) % 16), device_id_type=MESH
-        )
-    for o in range(1, 8):
-        pl.semaphore_signal(barrier, inc=1, device_id=((retr + o) % 8, store), device_id_type=MESH)
+    peers = [(dx, 0, dz, 0) for dx in STEP for dz in STEP if dx or dz]
+    peers += [(0, dy, 0, dc) for dy in STEP for dc in (0, 1) if dy or dc]
+    for peer in sorted(peers, key=lambda p: -sum(map(abs, p))):
+        pl.semaphore_signal(barrier, inc=1, device_id=device(*peer), device_id_type=MESH)
     reqs[...] = jnp.zeros((8, 128), I32)
+    for copy in small:
+        copy.wait()
     reqs[0:2, 0:8] = shard_ref[...]
     reqs[2:4, 0:8] = slot_ref[...]
 
-    for copy in raws:
-        copy.wait()
-
-    def split(s, carry):
-        raw = kvraw[s].astype(F32)
-        one = jnp.where(c == 0, raw[:, 0, :], raw[:, 1, :])
-        kvsend[s] = jnp.concatenate([one, jnp.zeros((EPAD - EROWS, DH), F32)], axis=0).astype(BF16)
-        return carry
-
-    lax.fori_loop(0, 16, split, 0)
     pl.semaphore_wait(barrier, 22)
 
     RET = [(o // 2, o % 2) for o in range(8)]
@@ -142,6 +137,16 @@
         go(k, 0, 1)
         go(k, 0, 2)
 
+    for copy in raws:
+        copy.wait()
+
+    def split(s, carry):
+        raw = kvraw[s].astype(F32)
+        one = jnp.where(c == 0, raw[:, 0, :], raw[:, 1, :])
+        kvsend[s] = jnp.concatenate([one, jnp.zeros((EPAD - EROWS, DH), F32)], axis=0).astype(BF16)
+        return carry
+
+    lax.fori_loop(0, 16, split, 0)
     kv_msg = []
     for o in range(1, 16):
         to = (store + o) % 16
@@ -329,25 +334,20 @@
 
     for o in (1, 3, 5, 7):
         wy_msg[o].wait_recv()
-    for o in (2, 6):
+    for o in (1, 2, 6):
         pool_msg[o].wait_recv()
-    kv_blocks((retr, peer_from(2), peer_from(6)))
+    kv_blocks((retr, *(peer_from(o) for o in (1, 2, 6))))
     for k in range(2):
         for i in range(3):
             came(k, i, 3, 0)
             came(k, i, 3, 1)
     query_blocks(3, lambda t: (t, 3))
-    for k in range(2):
-        came(k, 3, 3, 0)
-        came(k, 3, 3, 1)
-    query_blocks(1, lambda t: (3, 3))
-    for group in ((4, 5), (1, 3, 7)):
-        for o in group:
-            if o in (4, 5):
-                share_msg(o).wait_recv()
-            else:
-                pool_msg[o].wait_recv()
-        kv_blocks(tuple(peer_from(o) for o in group))
+    for o in (4, 5):
+        share_msg(o).wait_recv()
+    kv_blocks((peer_from(4), peer_from(5)))
+    for o in (3, 7):
+        pool_msg[o].wait_recv()
+    kv_blocks((peer_from(3), peer_from(7)))
 
     def span(n, carry):
         rows = pl.ds(pl.multiple_of(n * SPAN, SPAN), SPAN)
@@ -401,13 +401,19 @@
         )
 
     FAR = (3, 1, 2, 0)
-    for k in range(2):
+    def far(k, i):
+        send1[k, i, 0] = block(k, STEP[i], 2).astype(BF16)
+        for h in range(2):
+            one_h(k, i, h).start()
+
+    for k in range(2):
+        came(k, 3, 3, 0)
+        came(k, 3, 3, 1)
+        query_block(k, 3, 3)
         lax.fori_loop(4 * k, 4 * k + 4, span, 0, unroll=4)
-        for i in FAR:
-            send1[k, i, 0] = block(k, STEP[i], 2).astype(BF16)
-            for h in range(2):
-                one_h(k, i, h).start()
-    for i in FAR:
+        for i in (3, 1):
+            far(k, i)
+    def to_neighbours(i):
         for k in range(2):
             for d in range(2):
                 one_h(k, i, d).wait_recv()
@@ -418,7 +424,7 @@
                 send1[k, i, 1 + d, at] = (part[d * QUART : (d + 1) * QUART] + got).astype(BF16)
                 send1[k, i, 1 + d, rest] = part[(1 - d) * QUART : (2 - d) * QUART].astype(BF16)
                 one(k, i, d).start()
-    for i in FAR:
+    def across(i):
         for k in range(2):
             for d in range(2):
                 one(k, i, d).wait_recv()
@@ -443,6 +449,19 @@
                 own = slots[k, 0, 0].astype(F32)
                 out_ref[pl.ds(k * HALF, HALF), :] = (own + total).astype(BF16)
 
+    to_neighbours(3)
+    for k in range(2):
+        far(k, 2)
+    to_neighbours(1)
+    across(3)
+    for k in range(2):
+        far(k, 0)
+    to_neighbours(2)
+    across(1)
+    to_neighbours(0)
+    across(2)
+    across(0)
+
     for msg in started:
         msg.wait_send()
     for msg in kv_msg:
@@ -472,7 +491,7 @@
     return pl.pallas_call(
         kernel,
         out_shape=jax.ShapeDtypeStruct((ROWS, HC), BF16),
-        in_specs=[hbm, vmem, vmem, vmem, hbm, hbm, hbm, hbm],
+        in_specs=[hbm] * 8,
         out_specs=vmem,
         scratch_shapes=[
             pltpu.VMEM((2, 4, 4, HALF, HC), BF16),
@@ -501,7 +520,10 @@
             pltpu.VMEM((2, 3, HALF, HC), BF16),
             pltpu.VMEM((2, 2, QUART, HC), BF16),
             pltpu.VMEM((2, 2, HALF, HC), BF16),
-            dma((6,)), dma((16,)), dma((2, 4, 4, 2)), dma((2, 4, 4, 2)), dma((8,)), dma((8,)),
+            pltpu.VMEM((16, 4, 128), F32),
+            pltpu.VMEM((2, 8), I32),
+            pltpu.VMEM((2, 8), I32),
+            dma((9,)), dma((16,)), dma((2, 4, 4, 2)), dma((2, 4, 4, 2)), dma((8,)), dma((8,)),
             dma((16,)), dma((16,)), dma((8,)), dma((8,)), dma((8,)), dma((8,)), dma((2,)), dma((2,)),
             dma((2, 4, 2)), dma((2, 4, 2)), dma((2, 4, 2)), dma((2, 4, 2)), dma((2, 4)), dma((2, 4)),
         ],

time: 120 us -> 113 us (0.942)
  Pallas kernels: 118 us -> 111 us
    pallas_call x1, Pallas kernels: 118 us -> 111 us  [on_device(): pl.pallas_call(kernel, out_shape=jax.ShapeDtypeStruct((ROWS, HC), BF16),...]
where the time goes in v3:
time: 113 us
  Pallas kernels  111 us (98%)
  local copies, waits for them, and re-layouts  1.87 us (2%)
    pallas_call x1, Pallas kernels, on_device(): pl.pallas_call(kernel, out_shape=jax.ShapeDtypeStruct((ROWS, HC), BF16),...  111 us

profile of v3, /device:TPU:1, one launch (start us, length us, event | category | flops | bytes accessed | tf_op | source)
XLA Modules:
  0.0 112.7 jit_solution(17844250200204513400)
XLA Ops:
  0.0 110.8 %retro_block.1 = bf16[512,512]{1,0:T(8,128)(2,1)} custom-call(bf16[512,512]{1,0:T(8,128)(2,1)} %tok_ref.1, f32[16,4,128]{2,1,0:T(4,128)} %bitcast.3, s32[2,8]{1,0:T(2,128)} %bitcast.4, s32[2,8]{1,0:T(2,128)} %bitcast.5, bf16[8192,512]{1,0:T(8,128)(2,1)} %wq_hbm.1, bf16[56,2,8192]{2,1,0:T(2,128)(2,1)} %kvw_hbm.1, bf16[512,8192]{1,0:T(8,128)(2,1)} %wo_hbm.1, ...), custom_call_target="tpu_custom_call" | custom-call | flops 12999999488 | bytes 24000000 | tf_op jit(solution)/shard_map/retro_block/pallas_call | solution.py:491
  110.8 1.9 %copy.10 = bf16[512,512]{1,0:T(8,128)(2,1)} copy(bf16[512,512]{1,0:T(8,128)(2,1)} %retro_block.1) | data formatting | bytes 1048576

commit v4 on v3

--- a/solution.py
+++ b/solution.py
@@ -23,7 +23,7 @@
     slots, wq, acc, ssq, pool, picked, fetched, keys, values, kvraw, kvsend, kvrecv, w32, wkv,
     reqs, table, table_s, place_s, att, wo, send1, recv1h, recv1, send2, recv2h, recv2,
     gain_ref, shard_ref, slot_ref, load_sem, raw_sem, ag_send, ag_recv, req_send, req_recv, kv_send, kv_recv,
-    wy_send, wy_recv, pool_send, pool_recv, share_send, share_recv, rs1h_send, rs1h_recv, rs1_send, rs1_recv,
+    wy_send, wy_recv, pool_send, pool_recv, share_send, share_recv, won_send, won_recv, rs1h_send, rs1h_recv, rs1_send, rs1_recv,
     rs2_send, rs2_recv,
 ):
     retr, store = lax.axis_index("retr"), lax.axis_index("store")
@@ -58,6 +58,11 @@
     ]
     for copy in [*small, loads[0], loads[1]]:
         copy.start()
+    barrier = pltpu.get_barrier_semaphore()
+    peers = [(dx, 0, dz, 0) for dx in STEP for dz in STEP if dx or dz]
+    peers += [(0, dy, 0, dc) for dy in STEP for dc in (0, 1) if dy or dc]
+    for peer in sorted(peers, key=lambda p: -sum(map(abs, p))):
+        pl.semaphore_signal(barrier, inc=1, device_id=device(*peer), device_id_type=MESH)
     raws = [
         pltpu.make_async_copy(
             kvw_hbm.at[:, :, pl.ds(s * HC + y * DH, DH)], kvraw.at[s], raw_sem.at[s]
@@ -68,12 +73,6 @@
         copy.start()
     for copy in loads[2:]:
         copy.start()
-
-    barrier = pltpu.get_barrier_semaphore()
-    peers = [(dx, 0, dz, 0) for dx in STEP for dz in STEP if dx or dz]
-    peers += [(0, dy, 0, dc) for dy in STEP for dc in (0, 1) if dy or dc]
-    for peer in sorted(peers, key=lambda p: -sum(map(abs, p))):
-        pl.semaphore_signal(barrier, inc=1, device_id=device(*peer), device_id_type=MESH)
     reqs[...] = jnp.zeros((8, 128), I32)
     for copy in small:
         copy.wait()
@@ -83,20 +82,12 @@
     pl.semaphore_wait(barrier, 22)
 
     RET = [(o // 2, o % 2) for o in range(8)]
-    EARLY, LATE = [4, 5, 2, 6], [3, 7, 1]
-    ORDER = EARLY + LATE
+    EARLY, LATE, LAST = [4, 5], [2, 6, 1], [3, 7]
+    ORDER = EARLY + LATE + LAST
 
     def peer_from(o):
         dy, dc = RET[o]
         return (y - dy + 4) % 4 * 2 + (c + dc) % 2
-
-    req_msg = {}
-    for o in ORDER:
-        req_msg[o] = pltpu.make_async_remote_copy(
-            reqs, table.at[retr], req_send.at[o], req_recv.at[o],
-            device_id=device(0, RET[o][0], 0, RET[o][1]), device_id_type=MESH,
-        )
-        req_msg[o].start()
 
     def gather_msg(k, i, j, h):
         axis = 2 if j else 1
@@ -133,6 +124,13 @@
     for k in range(2):
         go(k, 1, 0)
         go(k, 2, 0)
+    req_msg = {}
+    for o in ORDER:
+        req_msg[o] = pltpu.make_async_remote_copy(
+            reqs, table.at[retr], req_send.at[o], req_recv.at[o],
+            device_id=device(0, RET[o][0], 0, RET[o][1]), device_id_type=MESH,
+        )
+        req_msg[o].start()
     for k in range(2):
         go(k, 0, 1)
         go(k, 0, 2)
@@ -258,6 +256,14 @@
     def weight_part(dy, dc):
         return wkv.at[(c + dc) % 2, :, pl.ds(pl.multiple_of((y - dy + 4) % 4 * DH, DH), DH)]
 
+    def weight_on(h):
+        rows, cols = pl.ds(h * (ENC // 2), ENC // 2), pl.ds(pl.multiple_of((y + (3, 1)[h]) % 4 * DH, DH), DH)
+        part = wkv.at[c, rows, cols]
+        return pltpu.make_async_remote_copy(
+            part, part, won_send.at[h], won_recv.at[h],
+            device_id=device(0, (1, -1)[h], 0, 0), device_id_type=MESH,
+        )
+
     def weight_msg(o):
         dy, dc = RET[o]
         if dc:
@@ -276,7 +282,7 @@
         wy_msg[o] = weight_msg(o)
         wy_msg[o].start()
 
-    for o in (2, 6, 4, 1):
+    for o in (2, 6, 1):
         weight_go(o)
     for o in LATE:
         pool_msg[o].start()
@@ -305,14 +311,24 @@
         pool_msg[o].wait_recv()
         share_msg(o).start()
     for k in range(2):
+        came(k, 0, 3, 0)
+        came(k, 0, 3, 1)
+    query_blocks(1, lambda t: (0, 3))
+    for h in range(2):
+        wy_msg[(2, 6)[h]].wait_recv()
+        weight_on(h).start()
+        weight_go((3, 7)[h])
+    for o in LAST:
+        pool_msg[o].start()
+    for k in range(2):
         came(k, 3, 1)
         go(k, 3, 3, 0)
         came(k, 3, 2)
         go(k, 3, 3, 1)
     query_blocks(2, lambda t: (3, 1 + t))
-    for o in (2, 6, 4):
-        wy_msg[o].wait_recv()
-        weight_go(o + 1)
+    for h in range(2):
+        weight_on(h).wait_recv()
+    weight_go(5)
 
     def kv_block(r):
         ctx = fetched[pl.ds(2 * r, 2)].reshape(2 * NL, ENC)
@@ -338,10 +354,10 @@
         pool_msg[o].wait_recv()
     kv_blocks((retr, *(peer_from(o) for o in (1, 2, 6))))
     for k in range(2):
-        for i in range(3):
+        for i in (1, 2):
             came(k, i, 3, 0)
             came(k, i, 3, 1)
-    query_blocks(3, lambda t: (t, 3))
+    query_blocks(2, lambda t: (1 + t, 3))
     for o in (4, 5):
         share_msg(o).wait_recv()
     kv_blocks((peer_from(4), peer_from(5)))
@@ -411,13 +427,14 @@
         came(k, 3, 3, 1)
         query_block(k, 3, 3)
         lax.fori_loop(4 * k, 4 * k + 4, span, 0, unroll=4)
-        for i in (3, 1):
-            far(k, i)
+        far(k, 3)
+    for k in range(2):
+        far(k, 1)
     def to_neighbours(i):
         for k in range(2):
             for d in range(2):
+                part = block(k, STEP[i], 1 if d == 0 else -1)
                 one_h(k, i, d).wait_recv()
-                part = block(k, STEP[i], 1 if d == 0 else -1)
                 at = pl.ds(d * QUART, QUART)
                 rest = pl.ds((1 - d) * QUART, QUART)
                 got = recv1h[k, i, d].astype(F32)
@@ -426,9 +443,10 @@
                 one(k, i, d).start()
     def across(i):
         for k in range(2):
+            total = acc[pl.ds(k * HALF, HALF), :] if i == 0 else block(k, STEP[i], 0)
             for d in range(2):
                 one(k, i, d).wait_recv()
-            total = block(k, STEP[i], 0) + recv1[k, i, 0].astype(F32) + recv1[k, i, 1].astype(F32)
+            total = total + recv1[k, i, 0].astype(F32) + recv1[k, i, 1].astype(F32)
             if i == 3:
                 send2[k, 0] = total.astype(BF16)
                 for h in range(2):
@@ -446,8 +464,7 @@
                 for d in range(2):
                     two(k, d).wait_recv()
                 total = total + recv2[k, 0].astype(F32) + recv2[k, 1].astype(F32)
-                own = slots[k, 0, 0].astype(F32)
-                out_ref[pl.ds(k * HALF, HALF), :] = (own + total).astype(BF16)
+                out_ref[pl.ds(k * HALF, HALF), :] = total.astype(BF16)
 
     to_neighbours(3)
     for k in range(2):
@@ -459,6 +476,8 @@
     to_neighbours(2)
     across(1)
     to_neighbours(0)
+    for k in range(2):
+        acc[pl.ds(k * HALF, HALF), :] = slots[k, 0, 0].astype(F32) + block(k, 0, 0)
     across(2)
     across(0)
 
@@ -469,9 +488,11 @@
     for o in ORDER:
         req_msg[o].wait_send()
         pool_msg[o].wait_send()
-        wy_msg[o].wait_send()
+        if o != 4:
+            wy_msg[o].wait_send()
     for o in (4, 5):
         share_msg(o).wait_send()
+        weight_on(o - 4).wait_send()
     for k in range(2):
         for i in range(4):
             for d in range(2):
@@ -524,7 +545,7 @@
             pltpu.VMEM((2, 8), I32),
             pltpu.VMEM((2, 8), I32),
             dma((9,)), dma((16,)), dma((2, 4, 4, 2)), dma((2, 4, 4, 2)), dma((8,)), dma((8,)),
-            dma((16,)), dma((16,)), dma((8,)), dma((8,)), dma((8,)), dma((8,)), dma((2,)), dma((2,)),
+            dma((16,)), dma((16,)), dma((8,)), dma((8,)), dma((8,)), dma((8,)), dma((2,)), dma((2,)), dma((2,)), dma((2,)),
             dma((2, 4, 2)), dma((2, 4, 2)), dma((2, 4, 2)), dma((2, 4, 2)), dma((2, 4)), dma((2, 4)),
         ],
         compiler_params=pltpu.CompilerParams(

time: 113 us -> 112 us (level)
  Pallas kernels: 111 us -> 109 us
    pallas_call x1, Pallas kernels: 111 us -> 109 us  [on_device(): pl.pallas_call(kernel, out_shape=jax.ShapeDtypeStruct((ROWS, HC), BF16),...]
where the time goes in v4:
time: 112 us; the launch traced here: 111 us
  Pallas kernels  109 us (97%)
  local copies, waits for them, and re-layouts  1.87 us (2%)
    pallas_call x1, Pallas kernels, on_device(): pl.pallas_call(kernel, out_shape=jax.ShapeDtypeStruct((ROWS, HC), BF16),...  109 us

profile of v4, /device:TPU:1, one launch (start us, length us, event | category | flops | bytes accessed | tf_op | source)
XLA Modules:
  0.0 111.4 jit_solution(1420249081970141011)
XLA Ops:
  0.0 109.5 %retro_block.1 = bf16[512,512]{1,0:T(8,128)(2,1)} custom-call(bf16[512,512]{1,0:T(8,128)(2,1)} %tok_ref.1, f32[16,4,128]{2,1,0:T(4,128)} %bitcast.3, s32[2,8]{1,0:T(2,128)} %bitcast.4, s32[2,8]{1,0:T(2,128)} %bitcast.5, bf16[8192,512]{1,0:T(8,128)(2,1)} %wq_hbm.1, bf16[56,2,8192]{2,1,0:T(2,128)(2,1)} %kvw_hbm.1, bf16[512,8192]{1,0:T(8,128)(2,1)} %wo_hbm.1, ...), custom_call_target="tpu_custom_call" | custom-call | flops 12999999488 | bytes 24000000 | tf_op jit(solution)/shard_map/retro_block/pallas_call | solution.py:512
  109.5 1.9 %copy.10 = bf16[512,512]{1,0:T(8,128)(2,1)} copy(bf16[512,512]{1,0:T(8,128)(2,1)} %retro_block.1) | data formatting | bytes 1048576

commit v5 on v4

--- a/solution.py
+++ b/solution.py
@@ -358,12 +358,12 @@
             came(k, i, 3, 0)
             came(k, i, 3, 1)
     query_blocks(2, lambda t: (1 + t, 3))
+    for o in (3, 7):
+        pool_msg[o].wait_recv()
+    kv_blocks((peer_from(3), peer_from(7)))
     for o in (4, 5):
         share_msg(o).wait_recv()
     kv_blocks((peer_from(4), peer_from(5)))
-    for o in (3, 7):
-        pool_msg[o].wait_recv()
-    kv_blocks((peer_from(3), peer_from(7)))
 
     def span(n, carry):
         rows = pl.ds(pl.multiple_of(n * SPAN, SPAN), SPAN)
@@ -441,6 +441,10 @@
                 send1[k, i, 1 + d, at] = (part[d * QUART : (d + 1) * QUART] + got).astype(BF16)
                 send1[k, i, 1 + d, rest] = part[(1 - d) * QUART : (2 - d) * QUART].astype(BF16)
                 one(k, i, d).start()
+    def result(k):
+        rows = pl.ds(k * HALF, HALF)
+        return pltpu.make_async_copy(att.at[rows], out_ref.at[rows], load_sem.at[k])
+
     def across(i):
         for k in range(2):
             total = acc[pl.ds(k * HALF, HALF), :] if i == 0 else block(k, STEP[i], 0)
@@ -464,7 +468,8 @@
                 for d in range(2):
                     two(k, d).wait_recv()
                 total = total + recv2[k, 0].astype(F32) + recv2[k, 1].astype(F32)
-                out_ref[pl.ds(k * HALF, HALF), :] = total.astype(BF16)
+                att[pl.ds(k * HALF, HALF), :] = total.astype(BF16)
+                result(k).start()
 
     to_neighbours(3)
     for k in range(2):
@@ -501,19 +506,21 @@
         for d in range(2):
             two_h(k, d).wait_send()
             two(k, d).wait_send()
+    for k in range(2):
+        result(k).wait()
 
 
 def on_device(
     tokens, norm_gain, query_weight, kv_weight, out_weight, neighbour_pool, neighbour_shard, neighbour_slot
 ):
     gain = norm_gain.reshape(16, 4, 128)
-    vmem, hbm = pl.BlockSpec(memory_space=pltpu.VMEM), pl.BlockSpec(memory_space=pl.ANY)
+    hbm = pl.BlockSpec(memory_space=pl.ANY)
     dma = pltpu.SemaphoreType.DMA
     return pl.pallas_call(
         kernel,
         out_shape=jax.ShapeDtypeStruct((ROWS, HC), BF16),
         in_specs=[hbm] * 8,
-        out_specs=vmem,
+        out_specs=hbm,
         scratch_shapes=[
             pltpu.VMEM((2, 4, 4, HALF, HC), BF16),
             pltpu.VMEM((D, HC), BF16),

time: 112 us -> 111 us (level)
  no operation moved by 1% of the time
where the time goes in v5:
time: 111 us
  Pallas kernels  109 us (98%)
  local copies, waits for them, and re-layouts  1.87 us (2%)
    pallas_call x1, Pallas kernels, on_device(): pl.pallas_call(kernel, out_shape=jax.ShapeDtypeStruct((ROWS, HC), BF16),...  109 us

profile of v5, /device:TPU:1, one launch (start us, length us, event | category | flops | bytes accessed | tf_op | source)
XLA Modules:
  0.0 110.9 jit_solution(10276567636735159230)
XLA Ops:
  0.0 109.1 %retro_block.1 = bf16[512,512]{1,0:T(8,128)(2,1)} custom-call(bf16[512,512]{1,0:T(8,128)(2,1)} %tok_ref.1, f32[16,4,128]{2,1,0:T(4,128)} %bitcast.3, s32[2,8]{1,0:T(2,128)} %bitcast.4, s32[2,8]{1,0:T(2,128)} %bitcast.5, bf16[8192,512]{1,0:T(8,128)(2,1)} %wq_hbm.1, bf16[56,2,8192]{2,1,0:T(2,128)(2,1)} %kvw_hbm.1, bf16[512,8192]{1,0:T(8,128)(2,1)} %wo_hbm.1, ...), custom_call_target="tpu_custom_call" | custom-call | flops 12999999488 | bytes 24000000 | tf_op jit(solution)/shard_map/retro_block/pallas_call | solution.py:519
  109.1 1.9 %copy.10 = bf16[512,512]{1,0:T(8,128)(2,1)} copy(bf16[512,512]{1,0:T(8,128)(2,1)} %retro_block.1) | data formatting | bytes 1048576
